TPU v7x, 32 devices: a whole 2x2x4 slice. The times are simulated.
32 devices in a mesh: dp: 8 (over z, y), tensor: 4 (over x, core).
Axes of the slice: x: 2, y: 2, z: 4, core: 2. Of those that a mesh axis runs over, the one named last changes fastest.
Arguments:
- residual: bfloat16 [1024, 2048], P(('dp', 'tensor')), may hold values from -6 to 6
- norm_gain: float32 [2048], replicated, may hold values from 0.1 to 1.9
- gate_weight: bfloat16 [2048, 7168], P(None, 'tensor'), may hold values from -0.125 to 0.125
- up_weight: bfloat16 [2048, 7168], P(None, 'tensor'), may hold values from -0.125 to 0.125
- hidden_grad: bfloat16 [1024, 7168], P('dp', 'tensor'), may hold values from -6 to 6
Outputs:
- residual_grad: bfloat16 [1024, 2048], P(('dp', 'tensor'))
- gate_weight_grad: bfloat16 [2048, 7168], P('dp', 'tensor')
- up_weight_grad: bfloat16 [2048, 7168], P('dp', 'tensor')
All inputs are finite; a program needn't handle non-finite values.
Results may differ from a plain program's by a relative error of at most 0.024.
Values may be sent and summed in bfloat16 or wider, within the bound.
A program may use at most 64 MiB of HBM per device.

v0:
```python
import jax
import jax.numpy as jnp
from jax import lax
from jax.sharding import PartitionSpec as P

EPSILON = 1e-05


def normalize(residual):
    values = residual.astype(jnp.float32)
    inverse = lax.rsqrt(jnp.mean(values * values, axis=-1, keepdims=True) + EPSILON)
    return (values * inverse, inverse)


def contract_last(left, right):
    return lax.dot_general(
        left, right, (((1,), (1,)), ((), ())), preferred_element_type=jnp.float32
    )


def contract_first(left, right):
    return lax.dot_general(
        left, right, (((0,), (0,)), ((), ())), preferred_element_type=jnp.float32
    )


def shards(residual, norm_gain, gate_weight, up_weight, hidden_grad):
    scaled, inverse = normalize(residual)
    gathered = lax.all_gather(residual, "tensor", axis=0, tiled=True)
    whole_scaled = normalize(gathered)[0]
    normed = (whole_scaled * norm_gain).astype(jnp.bfloat16)
    gate_value = jnp.dot(normed, gate_weight, preferred_element_type=jnp.float32)
    up_value = jnp.dot(normed, up_weight, preferred_element_type=jnp.float32)
    sigmoid_gate = jax.nn.sigmoid(gate_value)
    upstream = hidden_grad.astype(jnp.float32)
    up_grad = (upstream * gate_value * sigmoid_gate).astype(jnp.bfloat16)
    gate_grad = (
        upstream * up_value * sigmoid_gate * (1.0 + gate_value * (1.0 - sigmoid_gate))
    ).astype(jnp.bfloat16)
    normed_grad = lax.psum_scatter(
        (contract_last(gate_grad, gate_weight) + contract_last(up_grad, up_weight)).astype(
            jnp.bfloat16
        ),
        "tensor",
        scatter_dimension=0,
        tiled=True,
    ).astype(jnp.float32)
    weighted = normed_grad * norm_gain
    residual_grad = (
        (weighted - scaled * jnp.mean(weighted * scaled, axis=-1, keepdims=True)) * inverse
    ).astype(jnp.bfloat16)
    factor = float(normed.shape[0] * lax.axis_size("dp")) ** (-0.5)
    gate_part = contract_first(normed, gate_grad) * factor
    up_part = contract_first(normed, up_grad) * factor
    gate_total, up_total = (
        lax.psum_scatter(
            gate_part.astype(jnp.bfloat16), "dp", scatter_dimension=0, tiled=True
        ).astype(jnp.float32),
        lax.psum_scatter(
            up_part.astype(jnp.bfloat16), "dp", scatter_dimension=0, tiled=True
        ).astype(jnp.float32),
    )
    return (residual_grad, gate_total.astype(jnp.bfloat16), up_total.astype(jnp.bfloat16))


def solution(mesh):
    return jax.shard_map(
        shards,
        mesh=mesh,
        in_specs=(
            P(("dp", "tensor"), None),
            P(),
            P(None, "tensor"),
            P(None, "tensor"),
            P("dp", "tensor"),
        ),
        out_specs=(P(("dp", "tensor"), None), P("dp", "tensor"), P("dp", "tensor")),
        check_vma=False,
    )
```

profile of v0, /device:TPU:0, one launch (start us, length us, event | category | flops | bytes accessed | tf_op | source)
XLA Modules:
  0.0 332.7 jit_solution(14280317731443508031)
XLA Ops:
  7.2 0.0 reduce-scatter.4.cloned.1.call-start
  7.2 8.8 %all_gather.3 = bf16[128,2048]{1,0:T(8,128)(2,1)S(1)} all-gather(bf16[32,2048]{1,0:T(8,128)(2,1)} %param.5), channel_id=1, replica_groups=mesh['dp'=8,'tensor'=4] {'tensor'}, dimensions={0}, use_global_device_ids=true | all-gather | bytes 655360 | tf_op jit(solution)/shard_map/all_gather | solution.py:29
  16.0 0.2 fusion.4
  16.2 0.0 copy-start.1
  16.2 0.0 copy-start.2
  16.3 0.0 copy-start.3
  16.3 0.0 slice-start
  16.3 4.4 %fusion.18 = f32[128,1792]{1,0:T(8,128)S(1)} fusion(bf16[2048,1792]{1,0:T(8,128)(2,1)} %param.7, bf16[128,2048]{1,0:T(8,128)(2,1)S(1)} %all_gather.3, f32[2048]{0:T(1024)} %param.6, f32[128]{0:T(128)S(1)} %add_rsqrt_fusion.1), kind=kOutput, calls=%fused_computation.30 | convolution fusion | flops 940572672 | bytes 8790528 | tf_op jit(solution)/shard_map/dot_general | solution.py:32
  20.7 0.0 copy-done.1
  20.7 0.7 copy-done.2
  21.4 0.0 copy-done.3
  21.5 0.0 slice-start.1
  21.5 1.5 fusion.3
  23.0 0.0 slice-done
  23.0 0.9 slice-done.1
  23.9 2.5 fusion.23
  26.4 3.4 %fusion.2 = bf16[128,2048]{1,0:T(8,128)(2,1)} fusion(f32[128,2048]{1,0:T(8,128)S(1)} %fusion.23, bf16[2048,1792]{1,0:T(8,128)(2,1)S(1)} %copy-done.2, f32[128,1792]{1,0:T(8,128)S(1)} %fusion.18, bf16[128,1792]{1,0:T(8,128)(2,1)S(1)} %copy-done.3), kind=kOutput, calls=%fused_computation.6 | convolution fusion | flops 941654016 | bytes 10289152 | tf_op jit(solution)/shard_map/dot_general | solution.py:16
  29.7 0.0 reduce-scatter.4.cloned.1.call-update
  29.7 0.0 reduce-scatter.8.cloned.1.call-start
  29.8 5.2 %multiply_convert_fusion = bf16[2048,1792]{1,0:T(8,128)(2,1)} fusion(bf16[128,2048]{1,0:T(8,128)(2,1)S(1)} %all_gather.3, f32[2048]{0:T(1024)S(1)} %copy-done.1, f32[128]{0:T(128)S(1)} %add_rsqrt_fusion.1, f32[128,1792]{1,0:T(8,128)S(1)} %fusion.18, bf16[128,1792]{1,0:T(8,128)(2,1)S(1)} %copy-done.3), kind=kOutput, calls=%fused_computation | convolution fusion | flops 949518336 | bytes 9249280 | tf_op jit(solution)/shard_map/dot_general | solution.py:22
  35.0 0.0 reduce-scatter.8.cloned.1.call-update
  35.0 0.0 copy-start
  35.0 0.0 reduce-scatter.6.cloned.1.call-start
  35.1 5.2 %multiply_convert_fusion.1 = bf16[2048,1792]{1,0:T(8,128)(2,1)} fusion(bf16[128,1792]{1,0:T(8,128)(2,1)S(1)} %fusion.3, bf16[128,2048]{1,0:T(8,128)(2,1)S(1)} %all_gather.3, f32[2048]{0:T(1024)S(1)} %copy-done.1, f32[128]{0:T(128)S(1)} %add_rsqrt_fusion.1), kind=kOutput, calls=%fused_computation.1 | convolution fusion | flops 947912704 | bytes 8331776 | tf_op jit(solution)/shard_map/dot_general | solution.py:22
  40.2 0.0 reduce-scatter.6.cloned.1.call-update
  40.3 0.0 copy-done
  40.3 0.1 fusion.15
  40.4 12.0 %reduce-scatter.4.cloned.1.call-done = bf16[32,2048]{1,0:T(8,128)(2,1)} async-done(((bf16[128,2048]{1,0:T(8,128)(2,1)}), bf16[32,2048]{1,0:T(8,128)(2,1)}) %reduce-scatter.4.cloned.1.call-update) | async-done | bytes 131088 | tf_op jit(solution)/shard_map/reduce_scatter | solution.py:40
  52.4 1.1 fusion.11
  53.6 1.7 fusion.14
  55.2 134.5 %reduce-scatter.8.cloned.1.call-done = bf16[256,1792]{1,0:T(8,128)(2,1)} async-done(((bf16[2048,1792]{1,0:T(8,128)(2,1)}), bf16[256,1792]{1,0:T(8,128)(2,1)}) %reduce-scatter.8.cloned.1.call-update) | async-done | bytes 917520 | tf_op jit(solution)/shard_map/reduce_scatter | solution.py:59
  189.7 136.5 %reduce-scatter.6.cloned.1.call-done = bf16[256,1792]{1,0:T(8,128)(2,1)} async-done(((bf16[2048,1792]{1,0:T(8,128)(2,1)}), bf16[256,1792]{1,0:T(8,128)(2,1)}) %reduce-scatter.6.cloned.1.call-update) | async-done | bytes 917520 | tf_op jit(solution)/shard_map/reduce_scatter | solution.py:56
  (4 shorter events, 0.0 us)
Async XLA Ops:
  7.2 45.3 %reduce-scatter.4.cloned.1.call-start = ((), (), s32[]{:S(2)}) async-start(), calls=%async_computation.3 | async-start | bytes 655360 | tf_op jit(solution)/shard_map/reduce_scatter | solution.py:40
  16.2 4.5 %copy-start.1 = (f32[2048]{0:T(1024)S(1)}, f32[2048]{0:T(1024)}, u32[]{:S(2)}) copy-start(f32[2048]{0:T(1024)} %param.6) | copy-start | bytes 24580
  16.2 5.2 %copy-start.2 = (bf16[2048,1792]{1,0:T(8,128)(2,1)S(1)}, bf16[2048,1792]{1,0:T(8,128)(2,1)}, u32[]{:S(2)}) copy-start(bf16[2048,1792]{1,0:T(8,128)(2,1)} %param.8) | copy-start | bytes 22020100
  16.3 5.2 %copy-start.3 = (bf16[128,1792]{1,0:T(8,128)(2,1)S(1)}, bf16[128,1792]{1,0:T(8,128)(2,1)}, u32[]{:S(2)}) copy-start(bf16[128,1792]{1,0:T(8,128)(2,1)} %param.9) | copy-start | bytes 1376260
  16.3 6.7 %slice-start = ((s8[7340032]{0:T(1024)(128)(4,1)}), s8[4194304]{0:T(1024)(128)(4,1)S(1)}, s32[]{:S(2)}) async-start(s8[7340032]{0:T(1024)(128)(4,1)} %bitcast.6), calls=%async_computation.6 | async-start | bytes 8388608
  21.5 2.4 slice-start.1
  29.7 160.0 %reduce-scatter.8.cloned.1.call-start = ((), (), s32[]{:S(2)}) async-start(), calls=%async_computation.5 | async-start | bytes 8257536 | tf_op jit(solution)/shard_map/reduce_scatter | solution.py:59
  35.0 5.2 %copy-start = (bf16[32,2048]{1,0:T(8,128)(2,1)S(1)}, bf16[32,2048]{1,0:T(8,128)(2,1)}, u32[]{:S(2)}) copy-start(bf16[32,2048]{1,0:T(8,128)(2,1)} %param.5) | copy-start | bytes 393220
  35.0 291.2 %reduce-scatter.6.cloned.1.call-start = ((), (), s32[]{:S(2)}) async-start(), calls=%async_computation.4 | async-start | bytes 8257536 | tf_op jit(solution)/shard_map/reduce_scatter | solution.py:56
Sparse Core Ops, SparseCore 0:
  29.9 22.5 reduce-scatter.3
  57.0 132.6 reduce-scatter.7
  194.3 131.8 reduce-scatter.5
where the time goes:
time: 333 us
  waiting for transfers between devices  283 us (85%)
  matrix products  22.1 us (7%)
  between operations  13.8 us (4%)
  blocking collectives  8.83 us (3%)
    reduce_scatter x1, waiting for transfers between devices, shards(): lax.psum_scatter(gate_part.astype(jnp.bfloat16), 'dp', scatter_dimension=...  136 us
    reduce_scatter x1, waiting for transfers between devices, shards(): lax.psum_scatter(up_part.astype(jnp.bfloat16), 'dp', scatter_dimension=0,...  134 us
    reduce_scatter x1, waiting for transfers between devices, shards(): lax.psum_scatter((contract_last(gate_grad, gate_weight) + contract_last(u...  12 us
    dot_general x2, matrix products, contract_first(): lax.dot_general(left, right, (((0,), (0,)), ((), ())), preferred_element_...  10.4 us
    all_gather x1, blocking collectives, shards(): gathered = lax.all_gather(residual, 'tensor', axis=0, tiled=True)  8.83 us
  transfers between devices with their start and end apart: 3, of which 3 were waited for; matrix products, arithmetic and copies ran while one was open for 4% of the time, Pallas kernels for 0%

commit v1 on v0

--- a/solution.py
+++ b/solution.py
@@ -24,11 +24,7 @@
     )
 
 
-def shards(residual, norm_gain, gate_weight, up_weight, hidden_grad):
-    scaled, inverse = normalize(residual)
-    gathered = lax.all_gather(residual, "tensor", axis=0, tiled=True)
-    whole_scaled = normalize(gathered)[0]
-    normed = (whole_scaled * norm_gain).astype(jnp.bfloat16)
+def gate_grads(normed, gate_weight, up_weight, hidden_grad):
     gate_value = jnp.dot(normed, gate_weight, preferred_element_type=jnp.float32)
     up_value = jnp.dot(normed, up_weight, preferred_element_type=jnp.float32)
     sigmoid_gate = jax.nn.sigmoid(gate_value)
@@ -37,6 +33,19 @@
     gate_grad = (
         upstream * up_value * sigmoid_gate * (1.0 + gate_value * (1.0 - sigmoid_gate))
     ).astype(jnp.bfloat16)
+    return gate_grad, up_grad
+
+
+def shards(residual, norm_gain, gate_weight, up_weight, hidden_grad):
+    rows = hidden_grad.shape[0]
+    depth = residual.shape[1] // lax.axis_size("dp")
+    me = lax.axis_index("dp")
+    whole = lax.all_gather(residual, ("dp", "tensor"), axis=0, tiled=True)
+    upstream = lax.all_gather(hidden_grad, "dp", axis=0, tiled=True)
+    scaled, inverse = normalize(residual)
+    own_rows = lax.dynamic_slice_in_dim(whole, me * rows, rows, 0)
+    own_normed = (normalize(own_rows)[0] * norm_gain).astype(jnp.bfloat16)
+    gate_grad, up_grad = gate_grads(own_normed, gate_weight, up_weight, hidden_grad)
     normed_grad = lax.psum_scatter(
         (contract_last(gate_grad, gate_weight) + contract_last(up_grad, up_weight)).astype(
             jnp.bfloat16
@@ -49,17 +58,12 @@
     residual_grad = (
         (weighted - scaled * jnp.mean(weighted * scaled, axis=-1, keepdims=True)) * inverse
     ).astype(jnp.bfloat16)
-    factor = float(normed.shape[0] * lax.axis_size("dp")) ** (-0.5)
-    gate_part = contract_first(normed, gate_grad) * factor
-    up_part = contract_first(normed, up_grad) * factor
-    gate_total, up_total = (
-        lax.psum_scatter(
-            gate_part.astype(jnp.bfloat16), "dp", scatter_dimension=0, tiled=True
-        ).astype(jnp.float32),
-        lax.psum_scatter(
-            up_part.astype(jnp.bfloat16), "dp", scatter_dimension=0, tiled=True
-        ).astype(jnp.float32),
-    )
+    factor = float(whole.shape[0]) ** (-0.5)
+    normed = (normalize(whole)[0] * norm_gain).astype(jnp.bfloat16)
+    gate_all, up_all = gate_grads(normed, gate_weight, up_weight, upstream)
+    mine = lax.dynamic_slice_in_dim(normed, me * depth, depth, 1)
+    gate_total = contract_first(mine, gate_all) * factor
+    up_total = contract_first(mine, up_all) * factor
     return (residual_grad, gate_total.astype(jnp.bfloat16), up_total.astype(jnp.bfloat16))
 
 

time: 333 us -> 180 us (0.54)
  waiting for transfers between devices: 283 us -> 92 us
  matrix products: 22.1 us -> 59.9 us
  blocking collectives: 8.83 us -> 0 us
  other arithmetic: 3.15 us -> 11.4 us
    reduce_scatter x2 -> x0, waiting for transfers between devices: 271 us -> none  [the longest x1 136 us: shards(): lax.psum_scatter(gate_part.astype(jnp.bfloat16), 'dp', scatter_dimension=...]
    all_gather x0 -> x2, waiting for transfers between devices: none -> 90.6 us  [the longest x1 65.9 us: shards(): whole = lax.all_gather(residual, ('dp', 'tensor'), axis=0, tiled=True)]
    dot_general x2, matrix products: 10.4 us -> 26.7 us  [contract_first(): lax.dot_general(left, right, (((0,), (0,)), ((), ())), preferred_element_...]
    reduce_scatter x1, waiting for transfers between devices: 12 us -> 0.01 us  [shards(): lax.psum_scatter((contract_last(gate_grad, gate_weight) + contract_last(u...]
    dot_general x2, matrix products: 5.91 us -> 17.7 us  [gate_grads(): jnp.dot(normed, gate_weight, preferred_element_type=jnp.float32)]
    dot_general x2, matrix products: 5.81 us -> 15.5 us  [contract_last(): lax.dot_general(left, right, (((1,), (1,)), ((), ())), preferred_element_...]
    all_gather x1 -> x0, blocking collectives: 8.83 us -> none  [shards(): gathered = lax.all_gather(residual, 'tensor', axis=0, tiled=True)]
    reduce_sum x2 -> x3, other arithmetic: 0.32 us -> 5.34 us  [normalize(): jnp.mean(values * values, axis=-1, keepdims=True) + EPSILON]
  transfers between devices with their start and end apart: 3 -> 3, of which waited for: 3 -> 2; matrix products, arithmetic and copies ran while one was open for 4% -> 38% of each run, Pallas kernels for 0% -> 0%
where the time goes in v1:
time: 180 us; the launch traced here: 179 us
  waiting for transfers between devices  92 us (51%)
  matrix products  59.9 us (33%)
  between operations  13.8 us (8%)
  other arithmetic  11.4 us (6%)
  local copies, waits for them, and re-layouts  2.1 us (1%)
    all_gather x1, waiting for transfers between devices, shards(): whole = lax.all_gather(residual, ('dp', 'tensor'), axis=0, tiled=True)  65.9 us
    dot_general x2, matrix products, contract_first(): lax.dot_general(left, right, (((0,), (0,)), ((), ())), preferred_element_...  26.7 us
    all_gather x1, waiting for transfers between devices, shards(): upstream = lax.all_gather(hidden_grad, 'dp', axis=0, tiled=True)  24.7 us
    dot_general x2, matrix products, gate_grads(): jnp.dot(normed, gate_weight, preferred_element_type=jnp.float32)  17.7 us
    dot_general x2, matrix products, contract_last(): lax.dot_general(left, right, (((1,), (1,)), ((), ())), preferred_element_...  15.5 us
    reduce_sum x3, other arithmetic, normalize(): jnp.mean(values * values, axis=-1, keepdims=True) + EPSILON  5.34 us
  transfers between devices with their start and end apart: 3, of which 2 were waited for; matrix products, arithmetic and copies ran while one was open for 38% of the time, Pallas kernels for 0%

profile of v1, /device:TPU:0, one launch (start us, length us, event | category | flops | bytes accessed | tf_op | source)
XLA Modules:
  0.0 179.3 jit_solution(11523267741151784427)
XLA Ops:
  7.2 0.0 all-gather.3.cloned.1.call-start
  7.2 0.7 all-gather.3.cloned.1.call-update
  7.9 0.0 all-gather.5.cloned.1.call-start
  7.9 0.7 all-gather.5.cloned.1.call-update
  8.6 0.0 reduce-scatter.2.cloned.1.call-start
  8.7 1.0 fusion.38
  9.7 65.9 %all-gather.3.cloned.1.call-done = bf16[1024,2048]{1,0:T(8,128)(2,1)} async-done(((bf16[32,2048]{1,0:T(8,128)(2,1)}), bf16[1024,2048]{1,0:T(8,128)(2,1)}) %all-gather.3.cloned.1.call-update) | async-done | bytes 4194320 | tf_op jit(solution)/shard_map/all_gather | solution.py:43
  75.6 1.2 fusion.21
  76.9 3.1 %fusion = f32[1024]{0:T(1024)S(1)} fusion(bf16[1024,2048]{1,0:T(8,128)(2,1)} %all-gather.3.cloned.1.call-done), kind=kLoop, calls=%fused_computation.4 | loop fusion | flops 6290432 | bytes 4198400 | tf_op jit(solution)/shard_map/reduce_sum | solution.py:11
  80.0 0.0 copy-start.2
  80.0 0.0 copy-start.3
  80.0 4.5 %fusion.39 = f32[128,1792]{1,0:T(8,128)S(1)} fusion(bf16[2048,1792]{1,0:T(8,128)(2,1)} %param.7, f32[2048]{0:T(1024)} %param.6, f32[128]{0:T(128)S(1)} %add_rsqrt_fusion.2, bf16[1024,2048]{1,0:T(8,128)(2,1)} %all-gather.3.cloned.1.call-done, s32[]{:T(128)S(6)} %select_n.6), kind=kOutput, calls=%fused_computation.48 | convolution fusion | flops 940572672 | bytes 8790532 | tf_op jit(solution)/shard_map/dot_general | solution.py:28
  84.5 0.0 copy-done.2
  84.5 0.0 copy-done.3
  84.5 9.1 %fusion.26 = f32[128,2048]{1,0:T(8,128)S(1)} fusion(bf16[2048,1792]{1,0:T(8,128)(2,1)} %param.7, bf16[2048,1792]{1,0:T(8,128)(2,1)} %param.8, bf16[128,1792]{1,0:T(8,128)(2,1)S(1)} %copy-done.2, f32[128,1792]{1,0:T(8,128)S(1)} %fusion.39, f32[2048]{0:T(1024)S(1)} %copy-done.3, f32[128]{0:T(128)S(1)} %add_rsqrt_fusion.2, ...), kind=kOutput, calls=%fused_computation.33 | convolution fusion | flops 1882619904 | bytes 17637892 | tf_op jit(solution)/shard_map/dot_general | solution.py:16
  93.6 6.4 %fusion.19 = bf16[128,2048]{1,0:T(8,128)(2,1)} fusion(f32[128,2048]{1,0:T(8,128)S(1)} %fusion.26, bf16[2048,1792]{1,0:T(8,128)(2,1)} %param.8, f32[128,1792]{1,0:T(8,128)S(1)} %fusion.39, bf16[128,1792]{1,0:T(8,128)(2,1)S(1)} %copy-done.2), kind=kOutput, calls=%fused_computation.22 | convolution fusion | flops 941654016 | bytes 10289152 | tf_op jit(solution)/shard_map/dot_general | solution.py:16
  100.1 3.2 %fusion.2 = bf16[1024,2048]{1,0:T(8,128)(2,1)S(1)} fusion(bf16[1024,2048]{1,0:T(8,128)(2,1)} %all-gather.3.cloned.1.call-done, f32[2048]{0:T(1024)S(1)} %copy-done.3, f32[1024]{0:T(1024)S(1)} %add_rsqrt_fusion), kind=kLoop, calls=%fused_computation.6 | loop fusion | flops 8388608 | bytes 8400896 | tf_op jit(solution)/shard_map/convert_element_type | solution.py:62
  103.3 0.0 copy-start
  103.3 2.1 %copy-done = bf16[1024,2048]{1,0:T(8,128)(2,1)} copy-done((bf16[1024,2048]{1,0:T(8,128)(2,1)}, bf16[1024,2048]{1,0:T(8,128)(2,1)S(1)}, u32[]{:S(2)}) %copy-start) | copy-done | bytes 4194328
  105.3 13.2 %fusion.52 = f32[1024,1792]{1,0:T(8,128)} fusion(bf16[1024,2048]{1,0:T(8,128)(2,1)S(1)} %fusion.2, bf16[2048,1792]{1,0:T(8,128)(2,1)} %param.7), kind=kOutput, calls=%fused_computation.61 | convolution fusion | flops 7516192768 | bytes 18874368 | tf_op jit(solution)/shard_map/dot_general | solution.py:28
  118.5 0.0 reduce-scatter.2.cloned.1.call-update
  118.5 24.7 %all-gather.5.cloned.1.call-done = bf16[1024,1792]{1,0:T(8,128)(2,1)} async-done(((bf16[128,1792]{1,0:T(8,128)(2,1)}), bf16[1024,1792]{1,0:T(8,128)(2,1)}) %all-gather.5.cloned.1.call-update) | async-done | bytes 3670032 | tf_op jit(solution)/shard_map/all_gather | solution.py:44
  143.2 18.9 %fusion.13 = bf16[256,1792]{1,0:T(8,128)(2,1)} fusion(bf16[1024,1792]{1,0:T(8,128)(2,1)} %all-gather.5.cloned.1.call-done, f32[1024,1792]{1,0:T(8,128)} %fusion.52, bf16[1024,2048]{1,0:T(8,128)(2,1)} %copy-done, bf16[2048,1792]{1,0:T(8,128)(2,1)} %param.8, s32[]{:T(128)S(6)} %select_n.7), kind=kOutput, calls=%fused_computation.16 | convolution fusion | flops 8476819456 | bytes 23986180 | tf_op jit(solution)/shard_map/dot_general | solution.py:22
  162.1 0.0 copy-start.1
  162.1 7.8 %fusion.14 = bf16[256,1792]{1,0:T(8,128)(2,1)} fusion(f32[1024,1792]{1,0:T(8,128)} %fusion.52, bf16[1024,1792]{1,0:T(8,128)(2,1)} %all-gather.5.cloned.1.call-done, bf16[1024,2048]{1,0:T(8,128)(2,1)} %copy-done, s32[]{:T(128)S(6)} %select_n.7), kind=kOutput, calls=%fused_computation.17 | convolution fusion | flops 953286656 | bytes 12451844 | tf_op jit(solution)/shard_map/dot_general | solution.py:22
  169.9 0.0 reduce-scatter.2.cloned.1.call-done
  169.9 0.0 copy-done.1
  169.9 1.1 fusion.34
  171.1 1.7 fusion.37
  (4 shorter events, 0.0 us)
Async XLA Ops:
  7.2 68.5 %all-gather.3.cloned.1.call-start = ((), (), s32[]{:S(2)}) async-start(), calls=%async_computation.1 | async-start | bytes 4325376 | tf_op jit(solution)/shard_map/all_gather | solution.py:43
  7.9 135.3 %all-gather.5.cloned.1.call-start = ((), (), s32[]{:S(2)}) async-start(), calls=%async_computation.3 | async-start | bytes 4128768 | tf_op jit(solution)/shard_map/all_gather | solution.py:44
  8.6 161.3 %reduce-scatter.2.cloned.1.call-start = ((), (), s32[]{:S(2)}) async-start(), calls=%async_computation.2 | async-start | bytes 655360 | tf_op jit(solution)/shard_map/reduce_scatter | solution.py:49
  80.0 4.5 %copy-start.2 = (bf16[128,1792]{1,0:T(8,128)(2,1)S(1)}, bf16[128,1792]{1,0:T(8,128)(2,1)}, u32[]{:S(2)}) copy-start(bf16[128,1792]{1,0:T(8,128)(2,1)} %param.9) | copy-start | bytes 1376260
  80.0 4.5 %copy-start.3 = (f32[2048]{0:T(1024)S(1)}, f32[2048]{0:T(1024)}, u32[]{:S(2)}) copy-start(f32[2048]{0:T(1024)} %param.6) | copy-start | bytes 24580
  103.3 2.1 %copy-start = (bf16[1024,2048]{1,0:T(8,128)(2,1)}, bf16[1024,2048]{1,0:T(8,128)(2,1)S(1)}, u32[]{:S(2)}) copy-start(bf16[1024,2048]{1,0:T(8,128)(2,1)S(1)} %fusion.2) | copy-start | bytes 12582916
  162.1 7.8 %copy-start.1 = (bf16[32,2048]{1,0:T(8,128)(2,1)S(1)}, bf16[32,2048]{1,0:T(8,128)(2,1)}, u32[]{:S(2)}) copy-start(bf16[32,2048]{1,0:T(8,128)(2,1)} %param.5) | copy-start | bytes 393220
Sparse Core Ops, SparseCore 0:
  10.9 64.7 all-gather.2
  77.8 65.3 all-gather.4
  145.7 20.0 reduce-scatter.1

commit v2 on v1

--- a/solution.py
+++ b/solution.py
@@ -1,6 +1,8 @@
 import jax
 import jax.numpy as jnp
 from jax import lax
+from jax.experimental import pallas as pl
+from jax.experimental.pallas import tpu as pltpu
 from jax.sharding import PartitionSpec as P
 
 EPSILON = 1e-05
@@ -67,9 +69,330 @@
     return (residual_grad, gate_total.astype(jnp.bfloat16), up_total.astype(jnp.bfloat16))
 
 
+MESH = pl.DeviceIdType.MESH
+UP, DOWN, ACROSS = 0, 1, 2
+TILE = 256
+
+
+def fused_kernel(
+    res_ref, hid_ref, gain_ref, wg_hbm, wu_hbm,
+    dres_ref, dwg_ref, dwu_ref,
+    wg, wu, res, hid, normed, normed_t, gg, ug, accg, accu, part, parts,
+    wsem, lsem, dsend, drecv, msend, mrecv, psend, precv,
+):
+    me, t = lax.axis_index("dp"), lax.axis_index("tensor")
+    z, y = me // 2, me % 2
+    rows, wide = hid_ref.shape
+    slice_rows, features = res_ref.shape
+    depth = dwg_ref.shape[0]
+    half = rows // 2
+    tokens = res.shape[0]
+    factor = float(tokens) ** (-0.5)
+    last_z = tokens // rows // 2 - 1
+    n_tiles = wide // TILE
+    other = me + 1 - 2 * y
+    dest = {UP: me + 2, DOWN: me - 2, ACROSS: other}
+    order = [
+        z,
+        jnp.where(z == 0, 1, z - 1),
+        jnp.where(z < 2, 2, jnp.where(z == 2, 3, 1)),
+        jnp.where(z < 2, 3, 0),
+    ]
+
+    def place(g, p):
+        if p == 0:
+            start = pl.multiple_of(g * rows + t * slice_rows, slice_rows)
+            return res.at[pl.ds(start, slice_rows)]
+        start = pl.multiple_of(g * rows + (p - 1) * half, half)
+        return hid.at[pl.ds(start, half)]
+
+    def route(g, p, kind, own=False):
+        dst = place(g, p)
+        src = dst
+        if own:
+            src = res_ref if p == 0 else hid_ref.at[pl.ds((p - 1) * half, half)]
+        return pltpu.make_async_remote_copy(
+            src_ref=src, dst_ref=dst,
+            send_sem=dsend.at[g, p, kind], recv_sem=drecv.at[g, p],
+            device_id=(dest[kind], t), device_id_type=MESH,
+        )
+
+    def mate(g, k, own=False):
+        dst = place(g, 0)
+        return pltpu.make_async_remote_copy(
+            src_ref=res_ref if own else dst, dst_ref=dst,
+            send_sem=msend.at[g, k - 1], recv_sem=mrecv.at[g, k - 1],
+            device_id=(me, lax.rem(t + k, 4)), device_id_type=MESH,
+        )
+
+    def mates_start(g, own=False):
+        for k in (1, 2, 3):
+            mate(g, k, own).start()
+
+    def mates_wait(g):
+        for k in (1, 2, 3):
+            start = pl.multiple_of(g * rows + lax.rem(t + 4 - k, 4) * slice_rows, slice_rows)
+            pltpu.make_async_remote_copy(
+                src_ref=res.at[pl.ds(start, slice_rows)],
+                dst_ref=res.at[pl.ds(start, slice_rows)],
+                send_sem=msend.at[g, k - 1], recv_sem=mrecv.at[g, k - 1],
+                device_id=(me, lax.rem(t + k, 4)), device_id_type=MESH,
+            ).wait_recv()
+
+    def directions(j):
+        if j == 0:
+            return ((UP, z < last_z), (DOWN, z > 0))
+        below = order[j] < z
+        return (
+            (UP, jnp.logical_and(below, z < last_z)),
+            (DOWN, jnp.logical_and(jnp.logical_not(below), z > 0)),
+        )
+
+    def send(j, p):
+        g = order[j] * 2 + y
+        for kind, needed in directions(j):
+            @pl.when(needed)
+            def _():
+                route(g, p, kind, j == 0).start()
+        route(g, p, ACROSS, j == 0).start()
+        if p == 0 and j > 0:
+            mates_start(g)
+
+    def forward(j, p):
+        route(order[j] * 2 + y, p, ACROSS).wait_recv()
+        send(j, p)
+
+    def from_across(j, p):
+        g = order[j] * 2 + 1 - y
+        route(g, p, ACROSS).wait_recv()
+        if p == 0:
+            mates_start(g)
+
+    def norm_rows(zz, r0, count):
+        def body(i, carry):
+            at = pl.multiple_of(zz * 2 * rows + r0 + i * 32, 32)
+            values = res[pl.ds(at, 32), :].astype(jnp.float32)
+            inverse = lax.rsqrt(jnp.mean(values * values, axis=-1, keepdims=True) + EPSILON)
+            to = pl.multiple_of(r0 + i * 32, 32)
+            normed[pl.ds(to, 32), :] = (values * inverse * gain_ref[...]).astype(jnp.bfloat16)
+            return carry
+        lax.fori_loop(0, count // 32, body, 0)
+
+    def transpose_own():
+        columns = pl.ds(pl.multiple_of(me * depth, depth), depth)
+        normed_t[...] = normed[:, columns].astype(jnp.float32).T.astype(jnp.bfloat16)
+
+    def tiles(zz, r0, count, lo, hi, weigh=None):
+        def body(n, carry):
+            columns = pl.ds(pl.multiple_of(n * TILE, TILE), TILE)
+            there = pl.ds(pl.multiple_of(r0, rows), count)
+            left = normed[there, :]
+            gate = jnp.dot(left, wg[:, columns], preferred_element_type=jnp.float32)
+            up = jnp.dot(left, wu[:, columns], preferred_element_type=jnp.float32)
+            at = pl.ds(pl.multiple_of(zz * 2 * rows + r0, rows), count)
+            upstream = hid[at, columns].astype(jnp.float32)
+            sig = 0.5 * jnp.tanh(0.5 * gate) + 0.5
+            scaled_up = upstream * sig
+            ug[there, columns] = (scaled_up * gate).astype(jnp.bfloat16)
+            gg[there, columns] = (scaled_up * up * (1.0 + gate * (1.0 - sig))).astype(jnp.bfloat16)
+            if weigh is not None:
+                for acc, grad, out in ((accg, gg, dwg_ref), (accu, ug, dwu_ref)):
+                    term = jnp.dot(normed_t[...], grad[:, columns], preferred_element_type=jnp.float32)
+                    if weigh == "first":
+                        acc[:, columns] = term
+                    elif weigh == "more":
+                        acc[:, columns] += term
+                    else:
+                        out[:, columns] = ((acc[:, columns] + term) * factor).astype(out.dtype)
+            return carry
+        lax.fori_loop(lo, hi, body, 0)
+
+    def part_copy(k):
+        to = lax.rem(t + k, 4)
+        start = pl.multiple_of(to * slice_rows, slice_rows)
+        return pltpu.make_async_remote_copy(
+            src_ref=part.at[pl.ds(start, slice_rows)], dst_ref=parts.at[k - 1],
+            send_sem=psend.at[k - 1], recv_sem=precv.at[k - 1],
+            device_id=(me, to), device_id_type=MESH,
+        )
+
+    def back():
+        there = pl.ds(pl.multiple_of(y * rows, rows), rows)
+        def body(n, carry):
+            at = pl.ds(pl.multiple_of(n * TILE, TILE), TILE)
+            dims = (((1,), (1,)), ((), ()))
+            total = lax.dot_general(
+                gg[there, :], wg[at, :], dims, preferred_element_type=jnp.float32
+            ) + lax.dot_general(
+                ug[there, :], wu[at, :], dims, preferred_element_type=jnp.float32
+            )
+            part[:, at] = total.astype(jnp.bfloat16)
+            return carry
+        lax.fori_loop(0, features // TILE, body, 0)
+        for k in (1, 2, 3):
+            part_copy(k).start()
+
+    def finish_residual():
+        for k in (1, 2, 3):
+            part_copy(k).wait_recv()
+        own = part[pl.ds(pl.multiple_of(t * slice_rows, slice_rows), slice_rows), :]
+        total = own.astype(jnp.float32)
+        for k in (0, 1, 2):
+            total += parts[k].astype(jnp.float32)
+        values = res_ref[...].astype(jnp.float32)
+        inverse = lax.rsqrt(jnp.mean(values * values, axis=-1, keepdims=True) + EPSILON)
+        scaled = values * inverse
+        weighted = total * gain_ref[...]
+        mean = jnp.mean(weighted * scaled, axis=-1, keepdims=True)
+        dres_ref[...] = ((weighted - scaled * mean) * inverse).astype(dres_ref.dtype)
+
+    weights = [
+        pltpu.make_async_copy(wg_hbm, wg, wsem.at[0]),
+        pltpu.make_async_copy(wu_hbm, wu, wsem.at[1]),
+    ]
+    local = [
+        pltpu.make_async_copy(
+            res_ref, place(me, 0), lsem.at[0]
+        ),
+        pltpu.make_async_copy(
+            hid_ref, hid.at[pl.ds(pl.multiple_of(me * rows, rows), rows)], lsem.at[1]
+        ),
+    ]
+    for copy in weights + local:
+        copy.start()
+
+    barrier = pltpu.get_barrier_semaphore()
+    for kind, there in directions(0):
+        @pl.when(there)
+        def _():
+            pl.semaphore_signal(barrier, inc=1, device_id=(dest[kind], t), device_id_type=MESH)
+    pl.semaphore_signal(barrier, inc=1, device_id=(other, t), device_id_type=MESH)
+    for k in (1, 2, 3):
+        pl.semaphore_signal(
+            barrier, inc=1, device_id=(me, lax.rem(t + k, 4)), device_id_type=MESH
+        )
+    pl.semaphore_wait(
+        barrier, 4 + jnp.where(z > 0, 1, 0) + jnp.where(z < last_z, 1, 0)
+    )
+
+    mates_start(me, own=True)
+    for p in (0, 1, 2):
+        send(0, p)
+    for copy in local:
+        copy.wait()
+    mates_wait(me)
+    forward(1, 0)
+    norm_rows(z, y * rows, rows)
+    for copy in weights:
+        copy.wait()
+    split = n_tiles // 2 + 1
+    tiles(z, y * rows, rows, 0, split)
+    from_across(0, 0)
+    forward(1, 1)
+    tiles(z, y * rows, rows, split, n_tiles)
+    forward(1, 2)
+    back()
+    from_across(0, 1)
+    from_across(0, 2)
+    forward(2, 0)
+    mates_wait(other)
+    norm_rows(z, (1 - y) * rows, rows)
+    transpose_own()
+    tiles(z, (1 - y) * rows, rows, 0, split, "first")
+    from_across(1, 0)
+    forward(2, 1)
+    tiles(z, (1 - y) * rows, rows, split, n_tiles, "first")
+    forward(2, 2)
+
+    for j in (1, 2, 3):
+        zz = order[j]
+        if j == 2:
+            finish_residual()
+        from_across(j, 1)
+        if j == 1:
+            from_across(2, 0)
+        from_across(j, 2)
+        mates_wait(zz * 2)
+        mates_wait(zz * 2 + 1)
+        norm_rows(zz, 0, 2 * rows)
+        transpose_own()
+        weigh = "last" if j == 3 else "more"
+        if j == 1:
+            tiles(zz, 0, 2 * rows, 0, 3, weigh)
+            forward(3, 0)
+            tiles(zz, 0, 2 * rows, 3, 5, weigh)
+            forward(3, 1)
+            tiles(zz, 0, 2 * rows, 5, n_tiles, weigh)
+            forward(3, 2)
+            from_across(3, 0)
+        else:
+            tiles(zz, 0, 2 * rows, 0, n_tiles, weigh)
+
+    for j in range(4):
+        g = order[j] * 2 + y
+        for p in (0, 1, 2):
+            for kind, needed in directions(j):
+                @pl.when(needed)
+                def _():
+                    route(g, p, kind, j == 0).wait_send()
+            route(g, p, ACROSS, j == 0).wait_send()
+        for k in (1, 2, 3):
+            mate(g, k, j == 0).wait_send()
+            mate(order[j] * 2 + 1 - y, k).wait_send()
+    for k in (1, 2, 3):
+        part_copy(k).wait_send()
+
+
+def fused_shards(residual, norm_gain, gate_weight, up_weight, hidden_grad):
+    slice_rows, features = residual.shape
+    rows, wide = hidden_grad.shape
+    n_dp = lax.axis_size("dp")
+    depth = features // n_dp
+    vmem = pl.BlockSpec(memory_space=pltpu.VMEM)
+    hbm = pl.BlockSpec(memory_space=pl.ANY)
+    low, high = jnp.bfloat16, jnp.float32
+    dma = pltpu.SemaphoreType.DMA
+    return pl.pallas_call(
+        fused_kernel,
+        out_shape=(
+            jax.ShapeDtypeStruct((slice_rows, features), low),
+            jax.ShapeDtypeStruct((depth, wide), low),
+            jax.ShapeDtypeStruct((depth, wide), low),
+        ),
+        in_specs=[vmem, vmem, vmem, hbm, hbm],
+        out_specs=(vmem, vmem, vmem),
+        scratch_shapes=[
+            pltpu.VMEM((features, wide), low),
+            pltpu.VMEM((features, wide), low),
+            pltpu.VMEM((n_dp * rows, features), low),
+            pltpu.VMEM((n_dp * rows, wide), low),
+            pltpu.VMEM((2 * rows, features), low),
+            pltpu.VMEM((depth, 2 * rows), low),
+            pltpu.VMEM((2 * rows, wide), low),
+            pltpu.VMEM((2 * rows, wide), low),
+            pltpu.VMEM((depth, wide), high),
+            pltpu.VMEM((depth, wide), high),
+            pltpu.VMEM((rows, features), low),
+            pltpu.VMEM((3, slice_rows, features), low),
+            dma((2,)),
+            dma((2,)),
+            dma((n_dp, 3, 3)),
+            dma((n_dp, 3)),
+            dma((n_dp, 3)),
+            dma((n_dp, 3)),
+            dma((3,)),
+            dma((3,)),
+        ],
+        compiler_params=pltpu.CompilerParams(
+            collective_id=0, has_side_effects=True, vmem_limit_bytes=52 * 1024 * 1024
+        ),
+    )(residual, hidden_grad, norm_gain.reshape(1, features), gate_weight, up_weight)
+
+
 def solution(mesh):
+    fits = mesh.shape["dp"] == 8 and mesh.shape["tensor"] == 4
     return jax.shard_map(
-        shards,
+        fused_shards if fits else shards,
         mesh=mesh,
         in_specs=(
             P(("dp", "tensor"), None),

time: 180 us -> 85.6 us (0.48)
  waiting for transfers between devices: 92 us -> 0 us
  Pallas kernels: 0 us -> 77.3 us
  matrix products: 59.9 us -> 0 us
  between operations: 13.8 us -> 0.65 us
  other arithmetic: 11.4 us -> 0 us
  local copies, waits for them, and re-layouts: 2.1 us -> 6.35 us
    all_gather x2 -> x0, waiting for transfers between devices: 90.6 us -> none  [the longest x1 65.9 us: shards(): whole = lax.all_gather(residual, ('dp', 'tensor'), axis=0, tiled=True)]
    pallas_call x0 -> x1, Pallas kernels: none -> 77.3 us  [fused_shards(): pl.pallas_call(fused_kernel, out_shape=(jax.ShapeDtypeStruct((slice_rows,...]
    dot_general x6 -> x0, matrix products: 59.9 us -> none  [the longest x2 26.7 us: contract_first(): lax.dot_general(left, right, (((0,), (0,)), ((), ())), preferred_element_...]
    reduce_sum x4 -> x0, other arithmetic: 6.46 us -> none  [the longest x3 5.34 us: normalize(): jnp.mean(values * values, axis=-1, keepdims=True) + EPSILON]
    convert_element_type x2 -> x0, other arithmetic: 4.88 us -> none  [the longest x1 3.2 us: shards(): normed = (normalize(whole)[0] * norm_gain).astype(jnp.bfloat16)]
    unnamed x8 -> x9, local copies, waits for them, and re-layouts: 2.1 us -> 6.35 us
  transfers between devices with their start and end apart: 3 -> 0, of which waited for: 2 -> 0; matrix products, arithmetic and copies ran while one was open for 38% -> 0% of each run, Pallas kernels for 0% -> 0%
where the time goes in v2:
time: 85.6 us; the launch traced here: 84.3 us
  Pallas kernels  77.3 us (90%)
  local copies, waits for them, and re-layouts  6.35 us (7%)
    pallas_call x1, Pallas kernels, fused_shards(): pl.pallas_call(fused_kernel, out_shape=(jax.ShapeDtypeStruct((slice_rows,...  77.3 us
    unnamed x9, local copies, waits for them, and re-layouts  6.35 us

profile of v2, /device:TPU:0, one launch (start us, length us, event | category | flops | bytes accessed | tf_op | source)
XLA Modules:
  0.0 84.3 jit_solution(12493205658847831521)
XLA Ops:
  0.6 0.0 copy-start
  0.6 1.0 %copy-done = bf16[128,1792]{1,0:T(8,128)(2,1)S(1)} copy-done((bf16[128,1792]{1,0:T(8,128)(2,1)S(1)}, bf16[128,1792]{1,0:T(8,128)(2,1)}, u32[]{:S(2)}) %copy-start) | copy-done | bytes 458776
  1.7 0.0 copy-start.1
  1.7 0.9 %copy-done.1 = bf16[32,2048]{1,0:T(8,128)(2,1)S(1)} copy-done((bf16[32,2048]{1,0:T(8,128)(2,1)S(1)}, bf16[32,2048]{1,0:T(8,128)(2,1)}, u32[]{:S(2)}) %copy-start.1) | copy-done | bytes 131096
  2.6 0.0 copy-start.2
  2.6 0.7 copy-done.2
  3.3 77.3 %shard_map.76 = (bf16[32,2048]{1,0:T(8,128)(2,1)S(1)}, bf16[256,1792]{1,0:T(8,128)(2,1)S(1)}, bf16[256,1792]{1,0:T(8,128)(2,1)}) custom-call(bf16[32,2048]{1,0:T(8,128)(2,1)S(1)} %copy-done.1, bf16[128,1792]{1,0:T(8,128)(2,1)S(1)} %copy-done, f32[1,2048]{1,0:T(1,128)S(1)} %bitcast.1, bf16[2048,1792]{1,0:T(8,128)(2,1)} %wg_hbm.1, bf16[2048,1792]{1,0:T(8,128)(2,1)} %wu_hbm.1), custom_call_target="tpu_custom_call" | custom-call | tf_op jit(solution)/shard_map/pallas_call | solution.py:355
  80.5 0.7 copy.11
  81.2 0.9 %copy.12 = bf16[256,1792]{1,0:T(8,128)(2,1)} copy(bf16[256,1792]{1,0:T(8,128)(2,1)S(1)} %get-tuple-element.7) | data formatting | bytes 1835008
  82.1 2.2 %copy.13 = bf16[256,1792]{1,0:T(8,128)(2,1)} copy(bf16[256,1792]{1,0:T(8,128)(2,1)} %get-tuple-element.8) | data formatting | bytes 1835008
Async XLA Ops:
  0.6 1.0 %copy-start = (bf16[128,1792]{1,0:T(8,128)(2,1)S(1)}, bf16[128,1792]{1,0:T(8,128)(2,1)}, u32[]{:S(2)}) copy-start(bf16[128,1792]{1,0:T(8,128)(2,1)} %hid_ref.1) | copy-start | bytes 1376260
  1.7 0.9 %copy-start.1 = (bf16[32,2048]{1,0:T(8,128)(2,1)S(1)}, bf16[32,2048]{1,0:T(8,128)(2,1)}, u32[]{:S(2)}) copy-start(bf16[32,2048]{1,0:T(8,128)(2,1)} %res_ref.1) | copy-start | bytes 393220
  2.6 0.7 copy-start.2

commit v3 on v2

--- a/solution.py
+++ b/solution.py
@@ -75,9 +75,9 @@
 
 
 def fused_kernel(
-    res_ref, hid_ref, gain_ref, wg_hbm, wu_hbm,
+    res_ref, hid_ref, gain_hbm, wg_hbm, wu_hbm,
     dres_ref, dwg_ref, dwu_ref,
-    wg, wu, res, hid, normed, normed_t, gg, ug, accg, accu, part, parts,
+    gain_ref, silu, slope, wg, wu, res, hid, normed, normed_t, gg, ug, accg, accu, part, parts,
     wsem, lsem, dsend, drecv, msend, mrecv, psend, precv,
 ):
     me, t = lax.axis_index("dp"), lax.axis_index("tensor")
@@ -87,7 +87,6 @@
     depth = dwg_ref.shape[0]
     half = rows // 2
     tokens = res.shape[0]
-    factor = float(tokens) ** (-0.5)
     last_z = tokens // rows // 2 - 1
     n_tiles = wide // TILE
     other = me + 1 - 2 * y
@@ -182,19 +181,27 @@
         columns = pl.ds(pl.multiple_of(me * depth, depth), depth)
         normed_t[...] = normed[:, columns].astype(jnp.float32).T.astype(jnp.bfloat16)
 
-    def tiles(zz, r0, count, lo, hi, weigh=None):
+    def factors(zz, r0, count, lo, hi):
         def body(n, carry):
             columns = pl.ds(pl.multiple_of(n * TILE, TILE), TILE)
             there = pl.ds(pl.multiple_of(r0, rows), count)
             left = normed[there, :]
             gate = jnp.dot(left, wg[:, columns], preferred_element_type=jnp.float32)
             up = jnp.dot(left, wu[:, columns], preferred_element_type=jnp.float32)
+            sig = 0.5 * jnp.tanh(0.5 * gate) + 0.5
+            silu[there, columns] = gate * sig
+            slope[there, columns] = up * sig * (1.0 + gate * (1.0 - sig))
+            return carry
+        lax.fori_loop(lo, hi, body, 0)
+
+    def weigh_tiles(zz, r0, count, weigh):
+        def body(n, carry):
+            columns = pl.ds(pl.multiple_of(n * TILE, TILE), TILE)
+            there = pl.ds(pl.multiple_of(r0, rows), count)
             at = pl.ds(pl.multiple_of(zz * 2 * rows + r0, rows), count)
             upstream = hid[at, columns].astype(jnp.float32)
-            sig = 0.5 * jnp.tanh(0.5 * gate) + 0.5
-            scaled_up = upstream * sig
-            ug[there, columns] = (scaled_up * gate).astype(jnp.bfloat16)
-            gg[there, columns] = (scaled_up * up * (1.0 + gate * (1.0 - sig))).astype(jnp.bfloat16)
+            ug[there, columns] = (upstream * silu[there, columns]).astype(jnp.bfloat16)
+            gg[there, columns] = (upstream * slope[there, columns]).astype(jnp.bfloat16)
             if weigh is not None:
                 for acc, grad, out in ((accg, gg, dwg_ref), (accu, ug, dwu_ref)):
                     term = jnp.dot(normed_t[...], grad[:, columns], preferred_element_type=jnp.float32)
@@ -203,9 +210,9 @@
                     elif weigh == "more":
                         acc[:, columns] += term
                     else:
-                        out[:, columns] = ((acc[:, columns] + term) * factor).astype(out.dtype)
+                        out[:, columns] = (acc[:, columns] + term).astype(out.dtype)
             return carry
-        lax.fori_loop(lo, hi, body, 0)
+        lax.fori_loop(0, n_tiles, body, 0)
 
     def part_copy(k):
         to = lax.rem(t + k, 4)
@@ -239,7 +246,8 @@
         total = own.astype(jnp.float32)
         for k in (0, 1, 2):
             total += parts[k].astype(jnp.float32)
-        values = res_ref[...].astype(jnp.float32)
+        start = pl.multiple_of(me * rows + t * slice_rows, slice_rows)
+        values = res[pl.ds(start, slice_rows), :].astype(jnp.float32)
         inverse = lax.rsqrt(jnp.mean(values * values, axis=-1, keepdims=True) + EPSILON)
         scaled = values * inverse
         weighted = total * gain_ref[...]
@@ -257,8 +265,9 @@
         pltpu.make_async_copy(
             hid_ref, hid.at[pl.ds(pl.multiple_of(me * rows, rows), rows)], lsem.at[1]
         ),
+        pltpu.make_async_copy(gain_hbm, gain_ref, lsem.at[2]),
     ]
-    for copy in weights + local:
+    for copy in local + weights:
         copy.start()
 
     barrier = pltpu.get_barrier_semaphore()
@@ -275,58 +284,60 @@
         barrier, 4 + jnp.where(z > 0, 1, 0) + jnp.where(z < last_z, 1, 0)
     )
 
+    own_row, other_row = y * rows, (1 - y) * rows
     mates_start(me, own=True)
-    for p in (0, 1, 2):
-        send(0, p)
+    send(0, 0)
+    send(0, 1)
     for copy in local:
         copy.wait()
+    forward(1, 0)
+    from_across(0, 0)
+    send(0, 2)
     mates_wait(me)
-    forward(1, 0)
-    norm_rows(z, y * rows, rows)
+    norm_rows(z, own_row, rows)
     for copy in weights:
         copy.wait()
-    split = n_tiles // 2 + 1
-    tiles(z, y * rows, rows, 0, split)
-    from_across(0, 0)
+    factors(z, own_row, rows, 0, 2)
+    forward(2, 0)
+    factors(z, own_row, rows, 2, 4)
+    forward(3, 0)
+    from_across(1, 0)
+    factors(z, own_row, rows, 4, n_tiles)
     forward(1, 1)
-    tiles(z, y * rows, rows, split, n_tiles)
+    weigh_tiles(z, own_row, rows, None)
     forward(1, 2)
+    from_across(2, 0)
     back()
+    from_across(3, 0)
+    mates_wait(other)
+    norm_rows(z, other_row, rows)
+    factors(z, other_row, rows, 0, 4)
+    forward(2, 1)
+    factors(z, other_row, rows, 4, n_tiles)
     from_across(0, 1)
     from_across(0, 2)
-    forward(2, 0)
-    mates_wait(other)
-    norm_rows(z, (1 - y) * rows, rows)
     transpose_own()
-    tiles(z, (1 - y) * rows, rows, 0, split, "first")
-    from_across(1, 0)
-    forward(2, 1)
-    tiles(z, (1 - y) * rows, rows, split, n_tiles, "first")
-    forward(2, 2)
+    weigh_tiles(z, other_row, rows, "first")
 
     for j in (1, 2, 3):
         zz = order[j]
-        if j == 2:
-            finish_residual()
-        from_across(j, 1)
-        if j == 1:
-            from_across(2, 0)
-        from_across(j, 2)
         mates_wait(zz * 2)
         mates_wait(zz * 2 + 1)
         norm_rows(zz, 0, 2 * rows)
         transpose_own()
-        weigh = "last" if j == 3 else "more"
+        factors(zz, 0, 2 * rows, 0, 4)
         if j == 1:
-            tiles(zz, 0, 2 * rows, 0, 3, weigh)
-            forward(3, 0)
-            tiles(zz, 0, 2 * rows, 3, 5, weigh)
+            forward(2, 2)
+        if j == 2:
+            forward(3, 2)
+        factors(zz, 0, 2 * rows, 4, n_tiles)
+        if j == 1:
             forward(3, 1)
-            tiles(zz, 0, 2 * rows, 5, n_tiles, weigh)
-            forward(3, 2)
-            from_across(3, 0)
-        else:
-            tiles(zz, 0, 2 * rows, 0, n_tiles, weigh)
+        if j == 3:
+            finish_residual()
+        from_across(j, 1)
+        from_across(j, 2)
+        weigh_tiles(zz, 0, 2 * rows, "last" if j == 3 else "more")
 
     for j in range(4):
         g = order[j] * 2 + y
@@ -349,19 +360,22 @@
     n_dp = lax.axis_size("dp")
     depth = features // n_dp
     vmem = pl.BlockSpec(memory_space=pltpu.VMEM)
-    hbm = pl.BlockSpec(memory_space=pl.ANY)
+    hbm = pl.BlockSpec(memory_space=pltpu.HBM)
     low, high = jnp.bfloat16, jnp.float32
     dma = pltpu.SemaphoreType.DMA
-    return pl.pallas_call(
+    dres, dwg, dwu = pl.pallas_call(
         fused_kernel,
         out_shape=(
             jax.ShapeDtypeStruct((slice_rows, features), low),
             jax.ShapeDtypeStruct((depth, wide), low),
             jax.ShapeDtypeStruct((depth, wide), low),
         ),
-        in_specs=[vmem, vmem, vmem, hbm, hbm],
+        in_specs=[hbm] * 5,
         out_specs=(vmem, vmem, vmem),
         scratch_shapes=[
+            pltpu.VMEM((1, features), high),
+            pltpu.VMEM((2 * rows, wide), high),
+            pltpu.VMEM((2 * rows, wide), high),
             pltpu.VMEM((features, wide), low),
             pltpu.VMEM((features, wide), low),
             pltpu.VMEM((n_dp * rows, features), low),
@@ -375,7 +389,7 @@
             pltpu.VMEM((rows, features), low),
             pltpu.VMEM((3, slice_rows, features), low),
             dma((2,)),
-            dma((2,)),
+            dma((3,)),
             dma((n_dp, 3, 3)),
             dma((n_dp, 3)),
             dma((n_dp, 3)),
@@ -384,9 +398,12 @@
             dma((3,)),
         ],
         compiler_params=pltpu.CompilerParams(
-            collective_id=0, has_side_effects=True, vmem_limit_bytes=52 * 1024 * 1024
+            collective_id=0, has_side_effects=True, vmem_limit_bytes=56 * 1024 * 1024
         ),
     )(residual, hidden_grad, norm_gain.reshape(1, features), gate_weight, up_weight)
+    factor = float(n_dp * rows) ** (-0.5)
+    scale = lambda total: (total.astype(high) * factor).astype(low)
+    return dres, scale(dwg), scale(dwu)
 
 
 def solution(mesh):

time: 85.6 us -> 81.3 us (0.950)
  the two profiles are of different devices: /device:TPU:0 before, /device:TPU:1 now
where the time goes in v3:
time: 81.3 us; the launch traced here: 81.1 us
  Pallas kernels  76.8 us (94%)
  other arithmetic  3.01 us (4%)
    pallas_call x1, Pallas kernels, fused_shards(): pl.pallas_call(fused_kernel, out_shape=(jax.ShapeDtypeStruct((slice_rows,...  76.8 us
    convert_element_type x1, other arithmetic, fused_shards(): scale = lambda total: (total.astype(high) * factor).astype(low)  3.01 us

profile of v3, /device:TPU:1, one launch (start us, length us, event | category | flops | bytes accessed | tf_op | source)
XLA Modules:
  0.0 81.1 jit_solution(9856018373243376576)
XLA Ops:
  0.6 76.8 %shard_map.76 = (bf16[32,2048]{1,0:T(8,128)(2,1)}, bf16[256,1792]{1,0:T(8,128)(2,1)}, bf16[256,1792]{1,0:T(8,128)(2,1)}) custom-call(bf16[32,2048]{1,0:T(8,128)(2,1)} %res_ref.1, bf16[128,1792]{1,0:T(8,128)(2,1)} %hid_ref.1, f32[1,2048]{1,0:T(1,128)} %bitcast.1, bf16[2048,1792]{1,0:T(8,128)(2,1)} %wg_hbm.1, bf16[2048,1792]{1,0:T(8,128)(2,1)} %wu_hbm.1), custom_call_target="tpu_custom_call" | custom-call | tf_op jit(solution)/shard_map/pallas_call | solution.py:366
  77.4 0.0 copy-start
  77.4 3.0 %multiply_convert_fusion = (bf16[256,1792]{1,0:T(8,128)(2,1)}, bf16[256,1792]{1,0:T(8,128)(2,1)}) fusion(bf16[256,1792]{1,0:T(8,128)(2,1)} %get-tuple-element.8, bf16[256,1792]{1,0:T(8,128)(2,1)} %get-tuple-element.7), kind=kLoop, calls=%fused_computation | loop fusion | flops 2752512 | bytes 3670016 | tf_op jit(solution)/shard_map/convert_element_type | solution.py:405
  80.4 0.0 copy-done
  80.4 0.7 copy.9
Async XLA Ops:
  77.4 3.0 %copy-start = (bf16[32,2048]{1,0:T(8,128)(2,1)S(1)}, bf16[32,2048]{1,0:T(8,128)(2,1)}, u32[]{:S(2)}) copy-start(bf16[32,2048]{1,0:T(8,128)(2,1)} %get-tuple-element.14) | copy-start | bytes 393220

commit v4 on v3

--- a/solution.py
+++ b/solution.py
@@ -161,6 +161,14 @@
         route(order[j] * 2 + y, p, ACROSS).wait_recv()
         send(j, p)
 
+    def forward_if(needed, j, p):
+        @pl.when(needed)
+        def _():
+            forward(j, p)
+
+    inner = jnp.logical_and(z > 0, z < last_z)
+    outer = jnp.logical_not(inner)
+
     def from_across(j, p):
         g = order[j] * 2 + 1 - y
         route(g, p, ACROSS).wait_recv()
@@ -192,7 +200,7 @@
             silu[there, columns] = gate * sig
             slope[there, columns] = up * sig * (1.0 + gate * (1.0 - sig))
             return carry
-        lax.fori_loop(lo, hi, body, 0)
+        lax.fori_loop(lo, hi, body, 0, unroll=True)
 
     def weigh_tiles(zz, r0, count, weigh):
         def body(n, carry):
@@ -212,7 +220,7 @@
                     else:
                         out[:, columns] = (acc[:, columns] + term).astype(out.dtype)
             return carry
-        lax.fori_loop(0, n_tiles, body, 0)
+        lax.fori_loop(0, n_tiles, body, 0, unroll=True)
 
     def part_copy(k):
         to = lax.rem(t + k, 4)
@@ -301,19 +309,24 @@
     forward(2, 0)
     factors(z, own_row, rows, 2, 4)
     forward(3, 0)
+    forward(1, 1)
+    forward_if(inner, 2, 1)
     from_across(1, 0)
     factors(z, own_row, rows, 4, n_tiles)
-    forward(1, 1)
+    forward(1, 2)
+    forward_if(inner, 2, 2)
+    from_across(2, 0)
     weigh_tiles(z, own_row, rows, None)
-    forward(1, 2)
-    from_across(2, 0)
     back()
     from_across(3, 0)
     mates_wait(other)
     norm_rows(z, other_row, rows)
     factors(z, other_row, rows, 0, 4)
-    forward(2, 1)
+    forward_if(outer, 2, 1)
+    forward_if(inner, 3, 1)
     factors(z, other_row, rows, 4, n_tiles)
+    forward_if(outer, 2, 2)
+    forward_if(inner, 3, 2)
     from_across(0, 1)
     from_across(0, 2)
     transpose_own()
@@ -327,12 +340,10 @@
         transpose_own()
         factors(zz, 0, 2 * rows, 0, 4)
         if j == 1:
-            forward(2, 2)
-        if j == 2:
-            forward(3, 2)
+            forward_if(outer, 3, 1)
         factors(zz, 0, 2 * rows, 4, n_tiles)
         if j == 1:
-            forward(3, 1)
+            forward_if(outer, 3, 2)
         if j == 3:
             finish_residual()
         from_across(j, 1)
@@ -398,7 +409,7 @@
             dma((3,)),
         ],
         compiler_params=pltpu.CompilerParams(
-            collective_id=0, has_side_effects=True, vmem_limit_bytes=56 * 1024 * 1024
+            collective_id=0, has_side_effects=True, vmem_limit_bytes=44 * 1024 * 1024
         ),
     )(residual, hidden_grad, norm_gain.reshape(1, features), gate_weight, up_weight)
     factor = float(n_dp * rows) ** (-0.5)

time: 81.3 us -> 72.4 us (0.89)
  the two profiles are of different devices: /device:TPU:1 before, /device:TPU:0 now
where the time goes in v4:
time: 72.4 us; the launch traced here: 71.1 us
  Pallas kernels  62.5 us (86%)
  local copies, waits for them, and re-layouts  6.37 us (9%)
  other arithmetic  1.53 us (2%)
    pallas_call x1, Pallas kernels, fused_shards(): pl.pallas_call(fused_kernel, out_shape=(jax.ShapeDtypeStruct((slice_rows,...  62.5 us
    unnamed x9, local copies, waits for them, and re-layouts  6.37 us
    convert_element_type x1, other arithmetic, fused_shards(): scale = lambda total: (total.astype(high) * factor).astype(low)  1.53 us

profile of v4, /device:TPU:0, one launch (start us, length us, event | category | flops | bytes accessed | tf_op | source)
XLA Modules:
  0.0 71.1 jit_solution(17929836536551089686)
XLA Ops:
  0.6 0.0 copy-start
  0.6 3.1 %copy-done = bf16[2048,1792]{1,0:T(8,128)(2,1)S(1)} copy-done((bf16[2048,1792]{1,0:T(8,128)(2,1)S(1)}, bf16[2048,1792]{1,0:T(8,128)(2,1)}, u32[]{:S(2)}) %copy-start) | copy-done | bytes 7340056
  3.7 0.0 copy-start.1
  3.7 1.0 %copy-done.1 = bf16[128,1792]{1,0:T(8,128)(2,1)S(1)} copy-done((bf16[128,1792]{1,0:T(8,128)(2,1)S(1)}, bf16[128,1792]{1,0:T(8,128)(2,1)}, u32[]{:S(2)}) %copy-start.1) | copy-done | bytes 458776
  4.8 0.0 copy-start.2
  4.8 0.9 %copy-done.2 = bf16[32,2048]{1,0:T(8,128)(2,1)S(1)} copy-done((bf16[32,2048]{1,0:T(8,128)(2,1)S(1)}, bf16[32,2048]{1,0:T(8,128)(2,1)}, u32[]{:S(2)}) %copy-start.2) | copy-done | bytes 131096
  5.7 0.0 copy-start.3
  5.7 0.7 copy-done.3
  6.4 62.5 %shard_map.76 = (bf16[32,2048]{1,0:T(8,128)(2,1)S(1)}, bf16[256,1792]{1,0:T(8,128)(2,1)S(1)}, bf16[256,1792]{1,0:T(8,128)(2,1)S(1)}) custom-call(bf16[32,2048]{1,0:T(8,128)(2,1)S(1)} %copy-done.2, bf16[128,1792]{1,0:T(8,128)(2,1)S(1)} %copy-done.1, f32[1,2048]{1,0:T(1,128)S(1)} %bitcast.1, bf16[2048,1792]{1,0:T(8,128)(2,1)S(1)} %copy-done, ...), custom_call_target="tpu_custom_call" | custom-call | tf_op jit(solution)/shard_map/pallas_call | solution.py:377
  68.9 1.5 %multiply_convert_fusion = (bf16[256,1792]{1,0:T(8,128)(2,1)}, bf16[256,1792]{1,0:T(8,128)(2,1)}) fusion(bf16[256,1792]{1,0:T(8,128)(2,1)S(1)} %get-tuple-element.8, bf16[256,1792]{1,0:T(8,128)(2,1)S(1)} %get-tuple-element.7), kind=kLoop, calls=%fused_computation | loop fusion | flops 2752512 | bytes 3670016 | tf_op jit(solution)/shard_map/convert_element_type | solution.py:416
  70.4 0.7 copy.9
Async XLA Ops:
  0.6 3.1 %copy-start = (bf16[2048,1792]{1,0:T(8,128)(2,1)S(1)}, bf16[2048,1792]{1,0:T(8,128)(2,1)}, u32[]{:S(2)}) copy-start(bf16[2048,1792]{1,0:T(8,128)(2,1)} %wg_hbm.1) | copy-start | bytes 22020100
  3.7 1.0 %copy-start.1 = (bf16[128,1792]{1,0:T(8,128)(2,1)S(1)}, bf16[128,1792]{1,0:T(8,128)(2,1)}, u32[]{:S(2)}) copy-start(bf16[128,1792]{1,0:T(8,128)(2,1)} %hid_ref.1) | copy-start | bytes 1376260
  4.8 0.9 %copy-start.2 = (bf16[32,2048]{1,0:T(8,128)(2,1)S(1)}, bf16[32,2048]{1,0:T(8,128)(2,1)}, u32[]{:S(2)}) copy-start(bf16[32,2048]{1,0:T(8,128)(2,1)} %res_ref.1) | copy-start | bytes 393220
  5.7 0.7 copy-start.3

commit v5 on v4

--- a/solution.py
+++ b/solution.py
@@ -147,13 +147,19 @@
             (DOWN, jnp.logical_and(jnp.logical_not(below), z > 0)),
         )
 
+    def by_line(j, p):
+        return j == 1 and p == 2
+
+    line = ((UP, z < last_z), (DOWN, z == 1))
+
     def send(j, p):
         g = order[j] * 2 + y
         for kind, needed in directions(j):
             @pl.when(needed)
             def _():
                 route(g, p, kind, j == 0).start()
-        route(g, p, ACROSS, j == 0).start()
+        if not by_line(j, p):
+            route(g, p, ACROSS, j == 0).start()
         if p == 0 and j > 0:
             mates_start(g)
 
@@ -174,6 +180,11 @@
         route(g, p, ACROSS).wait_recv()
         if p == 0:
             mates_start(g)
+        if (j, p) == (0, 2):
+            for kind, needed in line:
+                @pl.when(needed)
+                def _():
+                    route(g, p, kind).start()
 
     def norm_rows(zz, r0, count):
         def body(i, carry):
@@ -326,9 +337,9 @@
     forward_if(inner, 3, 1)
     factors(z, other_row, rows, 4, n_tiles)
     forward_if(outer, 2, 2)
-    forward_if(inner, 3, 2)
     from_across(0, 1)
     from_across(0, 2)
+    forward_if(inner, 3, 2)
     transpose_own()
     weigh_tiles(z, other_row, rows, "first")
 
@@ -357,10 +368,15 @@
                 @pl.when(needed)
                 def _():
                     route(g, p, kind, j == 0).wait_send()
-            route(g, p, ACROSS, j == 0).wait_send()
+            if not by_line(j, p):
+                route(g, p, ACROSS, j == 0).wait_send()
         for k in (1, 2, 3):
             mate(g, k, j == 0).wait_send()
             mate(order[j] * 2 + 1 - y, k).wait_send()
+    for kind, needed in line:
+        @pl.when(needed)
+        def _():
+            route(other, 2, kind).wait_send()
     for k in (1, 2, 3):
         part_copy(k).wait_send()
 
@@ -409,7 +425,7 @@
             dma((3,)),
         ],
         compiler_params=pltpu.CompilerParams(
-            collective_id=0, has_side_effects=True, vmem_limit_bytes=44 * 1024 * 1024
+            collective_id=0, has_side_effects=True, vmem_limit_bytes=56 * 1024 * 1024
         ),
     )(residual, hidden_grad, norm_gain.reshape(1, features), gate_weight, up_weight)
     factor = float(n_dp * rows) ** (-0.5)

time: 72.4 us -> 70.8 us (0.978); the launches traced: 71.1 us -> 70.6 us
  local copies, waits for them, and re-layouts: 6.37 us -> 0.66 us
  Pallas kernels: 62.5 us -> 66.3 us
  other arithmetic: 1.53 us -> 3.01 us
    unnamed x9 -> x3, local copies, waits for them, and re-layouts: 6.37 us -> 0.66 us
    pallas_call x1, Pallas kernels: 62.5 us -> 66.3 us  [fused_shards(): pl.pallas_call(fused_kernel, out_shape=(jax.ShapeDtypeStruct((slice_rows,...]
    convert_element_type x1, other arithmetic: 1.53 us -> 3.01 us  [fused_shards(): scale = lambda total: (total.astype(high) * factor).astype(low)]
where the time goes in v5:
time: 70.8 us; the launch traced here: 70.6 us
  Pallas kernels  66.3 us (94%)
  other arithmetic  3.01 us (4%)
    pallas_call x1, Pallas kernels, fused_shards(): pl.pallas_call(fused_kernel, out_shape=(jax.ShapeDtypeStruct((slice_rows,...  66.3 us
    convert_element_type x1, other arithmetic, fused_shards(): scale = lambda total: (total.astype(high) * factor).astype(low)  3.01 us

profile of v5, /device:TPU:0, one launch (start us, length us, event | category | flops | bytes accessed | tf_op | source)
XLA Modules:
  0.0 70.6 jit_solution(15374227933890703554)
XLA Ops:
  0.6 66.3 %shard_map.76 = (bf16[32,2048]{1,0:T(8,128)(2,1)}, bf16[256,1792]{1,0:T(8,128)(2,1)}, bf16[256,1792]{1,0:T(8,128)(2,1)}) custom-call(bf16[32,2048]{1,0:T(8,128)(2,1)} %res_ref.1, bf16[128,1792]{1,0:T(8,128)(2,1)} %hid_ref.1, f32[1,2048]{1,0:T(1,128)} %bitcast.1, bf16[2048,1792]{1,0:T(8,128)(2,1)} %wg_hbm.1, bf16[2048,1792]{1,0:T(8,128)(2,1)} %wu_hbm.1), custom_call_target="tpu_custom_call" | custom-call | tf_op jit(solution)/shard_map/pallas_call | solution.py:393
  66.9 0.0 copy-start
  66.9 3.0 %multiply_convert_fusion = (bf16[256,1792]{1,0:T(8,128)(2,1)}, bf16[256,1792]{1,0:T(8,128)(2,1)}) fusion(bf16[256,1792]{1,0:T(8,128)(2,1)} %get-tuple-element.8, bf16[256,1792]{1,0:T(8,128)(2,1)} %get-tuple-element.7), kind=kLoop, calls=%fused_computation | loop fusion | flops 2752512 | bytes 3670016 | tf_op jit(solution)/shard_map/convert_element_type | solution.py:432
  69.9 0.0 copy-done
  69.9 0.7 copy.9
Async XLA Ops:
  66.9 3.0 %copy-start = (bf16[32,2048]{1,0:T(8,128)(2,1)S(1)}, bf16[32,2048]{1,0:T(8,128)(2,1)}, u32[]{:S(2)}) copy-start(bf16[32,2048]{1,0:T(8,128)(2,1)} %get-tuple-element.14) | copy-start | bytes 393220
